TPU v7x, 128 devices: a whole 4x4x4 slice. The times are simulated.
128 devices in a mesh: wide: 32 (over y, z_lo, x), narrow: 4 (over z_hi, core).
Axes of the slice: x: 4, y: 4, z: 4 (z_hi: 2, z_lo: 2; z = z_hi * 2 + z_lo), core: 2. Of those that a mesh axis runs over, the one named last changes fastest.
Arguments:
- tokens: bfloat16 [65536, 1024], P(('wide', 'narrow')), may hold values from -6 to 6
- router: bfloat16 [1024, 256], replicated, may hold values from -3 to 3
- expert_in: bfloat16 [128, 1024, 2048], P(('wide', 'narrow')), may hold values from -0.1875 to 0.1875
- expert_out: bfloat16 [128, 2048, 1024], P(('wide', 'narrow')), may hold values from -0.125 to 0.125
- upstream: bfloat16 [65536, 1024], P(('wide', 'narrow')), may hold values from -6 to 6
Outputs:
- token_grad: bfloat16 [65536, 1024], P(('wide', 'narrow'))
- router_grad: float32 [1024, 256], replicated
- expert_in_grad: bfloat16 [128, 1024, 2048], P(('wide', 'narrow'))
- expert_out_grad: bfloat16 [128, 2048, 1024], P(('wide', 'narrow'))
All inputs are finite; a program needn't handle non-finite values.
Results may differ from a plain program's by a relative error of at most 0.0089.
Values may be sent and summed in bfloat16 or wider, within the bound.
A program may use at most 128 MiB of HBM per device.

v0:
```python
import math

import jax
import jax.numpy as jnp
from jax import lax
from jax.sharding import PartitionSpec as P

M = 256
P_SIZE = 2


root_two_pi = math.sqrt(2.0 / math.pi)
cubic_coef = 0.044715


def gelu_value(hidden):
    return 0.5 * hidden * (1.0 + jnp.tanh(root_two_pi * (hidden + cubic_coef * hidden**3)))


def gelu_slope(hidden):
    tangent = jnp.tanh(root_two_pi * (hidden + cubic_coef * hidden**3))
    return 0.5 * (1.0 + tangent) + 0.5 * hidden * (1.0 - tangent * tangent) * root_two_pi * (
        1.0 + 3.0 * cubic_coef * hidden * hidden
    )


def send_inputs(array):
    return lax.all_to_all(array, ("wide", "narrow"), split_axis=0, concat_axis=0, tiled=True)


def send_outputs(array):
    return lax.all_to_all(array, ("wide", "narrow"), split_axis=0, concat_axis=0, tiled=True)


def send_grads(array):
    return lax.all_to_all(array, ("wide", "narrow"), split_axis=0, concat_axis=0, tiled=True)


def send_returns(array):
    return lax.all_to_all(array, ("wide", "narrow"), split_axis=0, concat_axis=0, tiled=True)


def expert_forward(rows_in, first_weight, second_weight):
    hidden = jnp.dot(rows_in, first_weight, preferred_element_type=jnp.float32)
    active = gelu_value(hidden).astype(jnp.bfloat16)
    outputs = jnp.dot(active, second_weight, preferred_element_type=jnp.float32).astype(
        jnp.bfloat16
    )
    return (hidden, active, outputs)


def expert_backward(rows_in, rows_grad, hidden, active, first_weight, second_weight):
    active_grad = jnp.einsum(
        "rd,fd->rf", rows_grad, second_weight, preferred_element_type=jnp.float32
    )
    second_grad = jnp.einsum(
        "rf,rd->fd", active, rows_grad, preferred_element_type=jnp.float32
    ).astype(jnp.bfloat16)
    pre_grad = (active_grad * gelu_slope(hidden)).astype(jnp.bfloat16)
    first_grad = jnp.einsum(
        "rd,rf->df", rows_in, pre_grad, preferred_element_type=jnp.float32
    ).astype(jnp.bfloat16)
    slot_back = jnp.einsum(
        "rf,df->rd", pre_grad, first_weight, preferred_element_type=jnp.float32
    ).astype(jnp.bfloat16)
    return (first_grad, second_grad, slot_back)


def local(tokens, router, expert_in, expert_out, upstream):
    wide_count = lax.axis_size("wide")
    narrow_count = lax.axis_size("narrow")
    experts = wide_count * narrow_count
    images = tokens.shape[0] // M
    model_width = tokens.shape[1]
    slot_count = router.shape[1]
    tokens3 = tokens.reshape(images, M, model_width)
    upstream3 = upstream.reshape(images, M, model_width)
    logits = jnp.einsum("imd,ds->ims", tokens3, router, preferred_element_type=jnp.float32)
    dispatch = jax.nn.softmax(logits, axis=1)
    combine = jax.nn.softmax(logits, axis=2)
    dispatch_low = dispatch.astype(jnp.bfloat16).reshape(images, M, experts, P_SIZE)
    combine_low = combine.astype(jnp.bfloat16).reshape(images, M, experts, P_SIZE)
    slot_shape = (experts, images * P_SIZE, model_width)
    slot_in = (
        jnp.einsum("imep,imd->eipd", dispatch_low, tokens3, preferred_element_type=jnp.float32)
        .astype(jnp.bfloat16)
        .reshape(slot_shape)
    )
    slot_grad = (
        jnp.einsum("imep,imd->eipd", combine_low, upstream3, preferred_element_type=jnp.float32)
        .astype(jnp.bfloat16)
        .reshape(slot_shape)
    )
    first_weight = expert_in[0]
    second_weight = expert_out[0]
    rows_in = send_inputs(slot_in).reshape(-1, model_width)
    hidden, active, outputs = expert_forward(rows_in, first_weight, second_weight)
    slot_out = send_outputs(outputs.reshape(slot_shape))
    rows_grad = send_grads(slot_grad).reshape(-1, model_width)
    first_grad, second_grad, slot_back = expert_backward(
        rows_in, rows_grad, hidden, active, first_weight, second_weight
    )
    slot_return = send_returns(slot_back.reshape(slot_shape))
    out_four = slot_out.reshape(experts, images, P_SIZE, model_width)
    return_four = slot_return.reshape(experts, images, P_SIZE, model_width)
    dispatch_grad = jnp.einsum(
        "imd,eipd->imep", tokens3, return_four, preferred_element_type=jnp.float32
    ).reshape(images, M, slot_count)
    combine_grad = jnp.einsum(
        "imd,eipd->imep", upstream3, out_four, preferred_element_type=jnp.float32
    ).reshape(images, M, slot_count)
    logit_grad = dispatch * (
        dispatch_grad - jnp.sum(dispatch * dispatch_grad, axis=1, keepdims=True)
    )
    logit_grad = logit_grad + combine * (
        combine_grad - jnp.sum(combine * combine_grad, axis=2, keepdims=True)
    )
    logit_low = logit_grad.astype(jnp.bfloat16)
    token_grad = jnp.einsum(
        "imep,eipd->imd", dispatch_low, return_four, preferred_element_type=jnp.float32
    )
    token_grad = token_grad + jnp.einsum(
        "ims,ds->imd", logit_low, router, preferred_element_type=jnp.float32
    )
    token_grad = token_grad.astype(jnp.bfloat16).reshape(-1, model_width)
    router_part = jnp.einsum("imd,ims->ds", tokens3, logit_low, preferred_element_type=jnp.float32)
    router_grad = lax.psum(router_part, ("wide", "narrow"))
    return (token_grad, router_grad, first_grad[None], second_grad[None])


def solution(mesh):
    return jax.shard_map(
        local,
        mesh=mesh,
        in_specs=(
            P(("wide", "narrow"), None),
            P(),
            P(("wide", "narrow"), None, None),
            P(("wide", "narrow"), None, None),
            P(("wide", "narrow"), None),
        ),
        out_specs=(
            P(("wide", "narrow"), None),
            P(),
            P(("wide", "narrow"), None, None),
            P(("wide", "narrow"), None, None),
        ),
        check_vma=False,
    )
```

profile of v0, /device:TPU:1, one launch (start us, length us, event | category | flops | bytes accessed | tf_op | source)
XLA Modules:
  0.0 280.2 jit_solution(4268162931640412234)
XLA Ops:
  8.4 2.5 fusion.57
  13.5 11.5 %all-to-all-start.1 = ((bf16[128,4,1024]{2,1,0:T(4,128)(2,1)}), bf16[128,4,1024]{2,1,0:T(4,128)(2,1)S(1)}, u32[]{:S(2)}, u32[]{:S(2)}) async-start(bf16[128,4,1024]{2,1,0:T(4,128)(2,1)} %copy.23), calls=%async_computation.1 | async-start | bytes 2097152 | tf_op jit(solution)/shard_map/all_to_all | solution.py:28
  25.0 2.6 fusion.58
  32.5 11.4 %all-to-all-done.1 = bf16[128,4,1024]{2,1,0:T(4,128)(2,1)S(1)} async-done(((bf16[128,4,1024]{2,1,0:T(4,128)(2,1)}), bf16[128,4,1024]{2,1,0:T(4,128)(2,1)S(1)}, u32[]{:S(2)}, u32[]{:S(2)}) %all-to-all-start.1) | async-done | bytes 1048608 | tf_op jit(solution)/shard_map/all_to_all | solution.py:28
  43.9 5.7 %all-to-all-start = ((bf16[128,4,1024]{2,1,0:T(4,128)(2,1)}), bf16[128,4,1024]{2,1,0:T(4,128)(2,1)}, u32[]{:S(2)}, u32[]{:S(2)}) async-start(bf16[128,4,1024]{2,1,0:T(4,128)(2,1)} %copy.21), calls=%async_computation | async-start | bytes 2097152 | tf_op jit(solution)/shard_map/all_to_all | solution.py:36
  50.7 5.0 %fusion.17 = f32[512,2048]{1,0:T(8,128)S(1)} fusion(bf16[512,1024]{1,0:T(8,128)(2,1)} %reshape.66, bf16[1,1024,2048]{2,1,0:T(8,128)(2,1)} %param.7), kind=kOutput, calls=%fused_computation.19 | convolution fusion | flops 2147483648 | bytes 9437184 | tf_op jit(solution)/shard_map/dot_general | solution.py:44
  55.7 2.0 copy-done.6
  57.7 2.7 fusion.26
  61.6 6.7 %all-to-all-done = bf16[128,4,1024]{2,1,0:T(4,128)(2,1)} async-done(((bf16[128,4,1024]{2,1,0:T(4,128)(2,1)}), bf16[128,4,1024]{2,1,0:T(4,128)(2,1)}, u32[]{:S(2)}, u32[]{:S(2)}) %all-to-all-start) | async-done | bytes 1048608 | tf_op jit(solution)/shard_map/all_to_all | solution.py:36
  68.3 4.6 %all-to-all-start.3 = ((bf16[128,4,1024]{2,1,0:T(4,128)(2,1)}), bf16[128,4,1024]{2,1,0:T(4,128)(2,1)S(1)}, u32[]{:S(2)}, u32[]{:S(2)}) async-start(bf16[128,4,1024]{2,1,0:T(4,128)(2,1)} %reshape.70), calls=%async_computation.3 | async-start | bytes 2097152 | tf_op jit(solution)/shard_map/all_to_all | solution.py:32
  72.9 2.1 reshape.64
  75.1 8.1 %fusion.14 = bf16[512,2048]{1,0:T(8,128)(2,1)S(1)} fusion(f32[512,2048]{1,0:T(8,128)} %copy-done.6, bf16[512,1024]{1,0:T(8,128)(2,1)} %reshape.64, bf16[1,2048,1024]{2,1,0:T(8,128)(2,1)} %param.8), kind=kOutput, calls=%fused_computation.16 | convolution fusion | flops 2167406592 | bytes 11534336 | tf_op jit(solution)/shard_map/rd,fd->rf/dot_general | solution.py:53
  84.6 3.4 %fusion.29 = bf16[512,1024]{1,0:T(8,128)(2,1)} fusion(bf16[512,2048]{1,0:T(8,128)(2,1)S(1)} %fusion.14, bf16[1,1024,2048]{2,1,0:T(8,128)(2,1)S(1)} %copy-done.5), kind=kOutput, calls=%fused_computation.33 | convolution fusion | flops 2148007936 | bytes 7340032 | tf_op jit(solution)/shard_map/rf,df->rd/dot_general | solution.py:63
  87.9 2.3 reshape.67
  90.2 1.8 all-to-all-done.3
  92.0 8.5 %all-to-all-start.2 = ((bf16[128,4,1024]{2,1,0:T(4,128)(2,1)}), bf16[128,4,1024]{2,1,0:T(4,128)(2,1)}, u32[]{:S(2)}, u32[]{:S(2)}) async-start(bf16[128,4,1024]{2,1,0:T(4,128)(2,1)} %reshape.67), calls=%async_computation.2 | async-start | bytes 2097152 | tf_op jit(solution)/shard_map/all_to_all | solution.py:40
  100.8 6.5 %convert_bitcast_fusion.1 = bf16[1,1024,2048]{2,1,0:T(8,128)(2,1)} fusion(bf16[512,1024]{1,0:T(8,128)(2,1)} %reshape.66, bf16[512,2048]{1,0:T(8,128)(2,1)} %copy-done.8), kind=kOutput, calls=%fused_computation.26 | convolution fusion | flops 2149580800 | bytes 7340032 | tf_op jit(solution)/shard_map/rd,rf->df/dot_general | solution.py:60
  107.3 5.0 %convert_bitcast_fusion = bf16[1,2048,1024]{2,1,0:T(8,128)(2,1)} fusion(bf16[512,1024]{1,0:T(8,128)(2,1)S(1)} %copy-done.2, f32[512,2048]{1,0:T(8,128)S(1)} %copy-done.7), kind=kOutput, calls=%fused_computation.25 | convolution fusion | flops 2159017984 | bytes 9437184 | tf_op jit(solution)/shard_map/rf,rd->fd/dot_general | solution.py:56
  113.8 5.3 %all-to-all-done.2 = bf16[128,4,1024]{2,1,0:T(4,128)(2,1)} async-done(((bf16[128,4,1024]{2,1,0:T(4,128)(2,1)}), bf16[128,4,1024]{2,1,0:T(4,128)(2,1)}, u32[]{:S(2)}, u32[]{:S(2)}) %all-to-all-start.2) | async-done | bytes 1048608 | tf_op jit(solution)/shard_map/all_to_all | solution.py:40
  124.0 3.0 %convolution_bitcast_fusion = f32[1024,256]{0,1:T(8,128)} fusion(bf16[2,256,1024]{2,1,0:T(8,128)(2,1)S(1)} %bitcast.93, f32[2,256,256]{1,2,0:T(8,128)S(1)} %fusion.42, f32[2,256,256]{1,2,0:T(8,128)} %get-tuple-element.13, f32[2,256,256]{1,2,0:T(8,128)} %reshape.69), kind=kOutput, calls=%fused_computation.34 | convolution fusion | flops 269091584 | bytes 3670016 | tf_op jit(solution)/shard_map/imd,ims->ds/dot_general | solution.py:126
  127.1 1.8 fusion.67
  128.9 3.8 %fusion.25 = bf16[2,256,1024]{2,1,0:T(8,128)(2,1)} fusion(f32[2,256,1024,1]{2,1,3,0:T(8,128)} %fusion.67, f32[2,256,256]{1,2,0:T(8,128)S(1)} %fusion.42, f32[2,256,256]{1,2,0:T(8,128)} %get-tuple-element.13, f32[2,256,256]{1,2,0:T(8,128)} %reshape.69, bf16[1024,256]{1,0:T(8,128)(2,1)S(1)} %copy-done.3), kind=kOutput, calls=%fused_computation.29 | convolution fusion | flops 270140160 | bytes 5242880 | tf_op jit(solution)/shard_map/ims,ds->imd/dot_general | solution.py:122
  132.7 138.1 %all-reduce.2.cloned.1.call-done = f32[1024,256]{0,1:T(8,128)} async-done(((f32[1024,256]{0,1:T(8,128)}), f32[1024,256]{0,1:T(8,128)}) %all-reduce.2.cloned.1.call-update) | async-done | bytes 1048592 | tf_op jit(solution)/shard_map/psum | solution.py:127
  270.8 2.5 copy.30
  (37 shorter events, 19.1 us)
Async XLA Ops:
  7.2 1.2 copy-start
  11.7 17.6 %copy-start.1 = (bf16[512,1024]{1,0:T(8,128)(2,1)S(1)}, bf16[512,1024]{1,0:T(8,128)(2,1)}, u32[]{:S(2)}) copy-start(bf16[512,1024]{1,0:T(8,128)(2,1)} %param.9) | copy-start | bytes 3145732
  13.5 30.4 %all-to-all-start.1 = ((bf16[128,4,1024]{2,1,0:T(4,128)(2,1)}), bf16[128,4,1024]{2,1,0:T(4,128)(2,1)S(1)}, u32[]{:S(2)}, u32[]{:S(2)}) async-start(bf16[128,4,1024]{2,1,0:T(4,128)(2,1)} %copy.23), calls=%async_computation.1 | async-start | bytes 2097152 | tf_op jit(solution)/shard_map/all_to_all | solution.py:28
  43.9 24.4 %all-to-all-start = ((bf16[128,4,1024]{2,1,0:T(4,128)(2,1)}), bf16[128,4,1024]{2,1,0:T(4,128)(2,1)}, u32[]{:S(2)}, u32[]{:S(2)}) async-start(bf16[128,4,1024]{2,1,0:T(4,128)(2,1)} %copy.21), calls=%async_computation | async-start | bytes 2097152 | tf_op jit(solution)/shard_map/all_to_all | solution.py:36
  50.7 7.0 %copy-start.4 = (bf16[1,2048,1024]{2,1,0:T(8,128)(2,1)S(1)}, bf16[1,2048,1024]{2,1,0:T(8,128)(2,1)}, u32[]{:S(2)}) copy-start(bf16[1,2048,1024]{2,1,0:T(8,128)(2,1)} %param.8) | copy-start | bytes 12582916
  55.7 2.0 copy-start.6
  68.3 23.7 %all-to-all-start.3 = ((bf16[128,4,1024]{2,1,0:T(4,128)(2,1)}), bf16[128,4,1024]{2,1,0:T(4,128)(2,1)S(1)}, u32[]{:S(2)}, u32[]{:S(2)}) async-start(bf16[128,4,1024]{2,1,0:T(4,128)(2,1)} %reshape.70), calls=%async_computation.3 | async-start | bytes 2097152 | tf_op jit(solution)/shard_map/all_to_all | solution.py:32
  75.1 9.5 %copy-start.5 = (bf16[1,1024,2048]{2,1,0:T(8,128)(2,1)S(1)}, bf16[1,1024,2048]{2,1,0:T(8,128)(2,1)}, u32[]{:S(2)}) copy-start(bf16[1,1024,2048]{2,1,0:T(8,128)(2,1)} %param.7) | copy-start | bytes 12582916
  83.2 1.4 copy-start.8
  92.0 27.1 %all-to-all-start.2 = ((bf16[128,4,1024]{2,1,0:T(4,128)(2,1)}), bf16[128,4,1024]{2,1,0:T(4,128)(2,1)}, u32[]{:S(2)}, u32[]{:S(2)}) async-start(bf16[128,4,1024]{2,1,0:T(4,128)(2,1)} %reshape.67), calls=%async_computation.2 | async-start | bytes 2097152 | tf_op jit(solution)/shard_map/all_to_all | solution.py:40
  100.5 170.3 %all-reduce.2.cloned.1.call-start = ((), (), s32[]{:S(2)}) async-start(), calls=%async_computation.4 | async-start | bytes 2097152 | tf_op jit(solution)/shard_map/psum | solution.py:127
  100.8 6.5 %copy-start.2 = (bf16[512,1024]{1,0:T(8,128)(2,1)S(1)}, bf16[512,1024]{1,0:T(8,128)(2,1)}, u32[]{:S(2)}) copy-start(bf16[512,1024]{1,0:T(8,128)(2,1)} %reshape.64) | copy-start | bytes 3145732
  100.8 6.5 %copy-start.7 = (f32[512,2048]{1,0:T(8,128)S(1)}, f32[512,2048]{1,0:T(8,128)}, u32[]{:S(2)}) copy-start(f32[512,2048]{1,0:T(8,128)} %copy-done.6) | copy-start | bytes 12582916
  124.0 4.9 %copy-start.3 = (bf16[1024,256]{1,0:T(8,128)(2,1)S(1)}, bf16[1024,256]{1,0:T(8,128)(2,1)}, u32[]{:S(2)}) copy-start(bf16[1024,256]{1,0:T(8,128)(2,1)} %param.6) | copy-start | bytes 1572868
Sparse Core Ops, SparseCore 0:
  127.2 143.5 all-reduce.1
where the time goes:
time: 281 us; the launch traced here: 280 us
  waiting for transfers between devices  163 us (58%)
  matrix products  47.1 us (17%)
  starting transfers between devices  30.6 us (11%)
  local copies, waits for them, and re-layouts  23.6 us (8%)
  between operations  14.2 us (5%)
    psum x1, waiting for transfers between devices, local(): router_grad = lax.psum(router_part, ('wide', 'narrow'))  138 us
    all_to_all x1, starting transfers between devices, send_inputs(): lax.all_to_all(array, ('wide', 'narrow'), split_axis=0, concat_axis=0, ti...  11.5 us
    all_to_all x1, waiting for transfers between devices, send_inputs(): lax.all_to_all(array, ('wide', 'narrow'), split_axis=0, concat_axis=0, ti...  11.4 us
    all_to_all x1, starting transfers between devices, send_returns(): lax.all_to_all(array, ('wide', 'narrow'), split_axis=0, concat_axis=0, ti...  8.55 us
    dot_general x1, matrix products, expert_backward(): jnp.einsum('rd,fd->rf', rows_grad, second_weight, preferred_element_type=...  8.14 us
    unnamed x19, local copies, waits for them, and re-layouts  7.14 us
    all_to_all x1, waiting for transfers between devices, send_grads(): lax.all_to_all(array, ('wide', 'narrow'), split_axis=0, concat_axis=0, ti...  6.68 us
    dot_general x1, matrix products, expert_backward(): jnp.einsum('rd,rf->df', rows_in, pre_grad, preferred_element_type=jnp.flo...  6.46 us
  transfers between devices with their start and end apart: 5, of which 5 were waited for; matrix products, arithmetic and copies ran while one was open for 19% of the time, Pallas kernels for 0%

commit v1 on v0

--- a/solution.py
+++ b/solution.py
@@ -123,8 +123,11 @@
         "ims,ds->imd", logit_low, router, preferred_element_type=jnp.float32
     )
     token_grad = token_grad.astype(jnp.bfloat16).reshape(-1, model_width)
-    router_part = jnp.einsum("imd,ims->ds", tokens3, logit_low, preferred_element_type=jnp.float32)
-    router_grad = lax.psum(router_part, ("wide", "narrow"))
+    router_part = jnp.einsum("ims,imd->sd", logit_low, tokens3, preferred_element_type=jnp.float32)
+    terms = send_inputs(router_part.astype(jnp.bfloat16).reshape(experts, P_SIZE, model_width))
+    own_rows = jnp.sum(terms.astype(jnp.float32), axis=0).astype(jnp.bfloat16)
+    rows = lax.all_gather(own_rows, ("wide", "narrow"), axis=0, tiled=True)
+    router_grad = rows.T.astype(jnp.float32)
     return (token_grad, router_grad, first_grad[None], second_grad[None])
 
 

time: 281 us -> 318 us (1.13)
  blocking collectives: 0 us -> 174 us
  waiting for transfers between devices: 163 us -> 33.4 us
  between operations: 14.2 us -> 0.83 us
  starting transfers between devices: 30.6 us -> 34.9 us
    all_gather x0 -> x1, blocking collectives: none -> 174 us  [local(): rows = lax.all_gather(own_rows, ('wide', 'narrow'), axis=0, tiled=True)]
    psum x1 -> x0, waiting for transfers between devices: 138 us -> none  [local(): router_grad = lax.psum(router_part, ('wide', 'narrow'))]
    all_to_all x1 -> x2, waiting for transfers between devices: 11.4 us -> 19.3 us  [send_inputs(): lax.all_to_all(array, ('wide', 'narrow'), split_axis=0, concat_axis=0, ti...]
    all_to_all x1 -> x2, starting transfers between devices: 11.5 us -> 16.1 us  [send_inputs(): lax.all_to_all(array, ('wide', 'narrow'), split_axis=0, concat_axis=0, ti...]
    unnamed x19 -> x17, local copies, waits for them, and re-layouts: 7.14 us -> 5.91 us
  transfers between devices with their start and end apart: 5 -> 5, of which waited for: 5 -> 5; matrix products, arithmetic and copies ran while one was open for 19% -> 16% of each run, Pallas kernels for 0% -> 0%
where the time goes in v1:
time: 318 us; the launch traced here: 317 us
  blocking collectives  174 us (55%)
  matrix products  46.2 us (15%)
  starting transfers between devices  34.9 us (11%)
  waiting for transfers between devices  33.4 us (11%)
  local copies, waits for them, and re-layouts  25.4 us (8%)
    all_gather x1, blocking collectives, local(): rows = lax.all_gather(own_rows, ('wide', 'narrow'), axis=0, tiled=True)  174 us
    all_to_all x2, waiting for transfers between devices, send_inputs(): lax.all_to_all(array, ('wide', 'narrow'), split_axis=0, concat_axis=0, ti...  19.3 us
    all_to_all x2, starting transfers between devices, send_inputs(): lax.all_to_all(array, ('wide', 'narrow'), split_axis=0, concat_axis=0, ti...  16.1 us
    all_to_all x1, starting transfers between devices, send_returns(): lax.all_to_all(array, ('wide', 'narrow'), split_axis=0, concat_axis=0, ti...  8.56 us
    dot_general x1, matrix products, expert_backward(): jnp.einsum('rd,fd->rf', rows_grad, second_weight, preferred_element_type=...  8.14 us
    all_to_all x1, waiting for transfers between devices, send_grads(): lax.all_to_all(array, ('wide', 'narrow'), split_axis=0, concat_axis=0, ti...  6.68 us
    dot_general x1, matrix products, expert_backward(): jnp.einsum('rd,rf->df', rows_in, pre_grad, preferred_element_type=jnp.flo...  6.46 us
  transfers between devices with their start and end apart: 5, of which 5 were waited for; matrix products, arithmetic and copies ran while one was open for 16% of the time, Pallas kernels for 0%

profile of v1, /device:TPU:1, one launch (start us, length us, event | category | flops | bytes accessed | tf_op | source)
XLA Modules:
  0.0 316.7 jit_solution(7113504222030328246)
XLA Ops:
  1.9 2.5 fusion.58
  6.9 11.5 %all-to-all-start.1 = ((bf16[128,4,1024]{2,1,0:T(4,128)(2,1)}), bf16[128,4,1024]{2,1,0:T(4,128)(2,1)S(1)}, u32[]{:S(2)}, u32[]{:S(2)}) async-start(bf16[128,4,1024]{2,1,0:T(4,128)(2,1)} %copy.34), calls=%async_computation.1 | async-start | bytes 2097152 | tf_op jit(solution)/shard_map/all_to_all | solution.py:28
  18.4 2.6 fusion.59
  25.9 11.4 %all-to-all-done.1 = bf16[128,4,1024]{2,1,0:T(4,128)(2,1)S(1)} async-done(((bf16[128,4,1024]{2,1,0:T(4,128)(2,1)}), bf16[128,4,1024]{2,1,0:T(4,128)(2,1)S(1)}, u32[]{:S(2)}, u32[]{:S(2)}) %all-to-all-start.1) | async-done | bytes 1048608 | tf_op jit(solution)/shard_map/all_to_all | solution.py:28
  37.4 5.7 %all-to-all-start = ((bf16[128,4,1024]{2,1,0:T(4,128)(2,1)}), bf16[128,4,1024]{2,1,0:T(4,128)(2,1)}, u32[]{:S(2)}, u32[]{:S(2)}) async-start(bf16[128,4,1024]{2,1,0:T(4,128)(2,1)} %copy.32), calls=%async_computation | async-start | bytes 2097152 | tf_op jit(solution)/shard_map/all_to_all | solution.py:36
  44.2 5.0 %fusion.17 = f32[512,2048]{1,0:T(8,128)S(1)} fusion(bf16[512,1024]{1,0:T(8,128)(2,1)} %reshape.69, bf16[1,1024,2048]{2,1,0:T(8,128)(2,1)} %param.7), kind=kOutput, calls=%fused_computation.19 | convolution fusion | flops 2147483648 | bytes 9437184 | tf_op jit(solution)/shard_map/dot_general | solution.py:44
  49.2 2.0 copy-done.5
  51.2 2.7 fusion.26
  55.1 6.7 %all-to-all-done = bf16[128,4,1024]{2,1,0:T(4,128)(2,1)} async-done(((bf16[128,4,1024]{2,1,0:T(4,128)(2,1)}), bf16[128,4,1024]{2,1,0:T(4,128)(2,1)}, u32[]{:S(2)}, u32[]{:S(2)}) %all-to-all-start) | async-done | bytes 1048608 | tf_op jit(solution)/shard_map/all_to_all | solution.py:36
  61.8 4.6 %all-to-all-start.3 = ((bf16[128,4,1024]{2,1,0:T(4,128)(2,1)}), bf16[128,4,1024]{2,1,0:T(4,128)(2,1)S(1)}, u32[]{:S(2)}, u32[]{:S(2)}) async-start(bf16[128,4,1024]{2,1,0:T(4,128)(2,1)} %reshape.73), calls=%async_computation.3 | async-start | bytes 2097152 | tf_op jit(solution)/shard_map/all_to_all | solution.py:32
  66.4 2.1 reshape.67
  68.5 8.1 %fusion.14 = bf16[512,2048]{1,0:T(8,128)(2,1)S(1)} fusion(f32[512,2048]{1,0:T(8,128)} %copy-done.5, bf16[512,1024]{1,0:T(8,128)(2,1)} %reshape.67, bf16[1,2048,1024]{2,1,0:T(8,128)(2,1)} %param.8), kind=kOutput, calls=%fused_computation.16 | convolution fusion | flops 2167406592 | bytes 11534336 | tf_op jit(solution)/shard_map/rd,fd->rf/dot_general | solution.py:53
  78.0 3.4 %fusion.29 = bf16[512,1024]{1,0:T(8,128)(2,1)} fusion(bf16[512,2048]{1,0:T(8,128)(2,1)S(1)} %fusion.14, bf16[1,1024,2048]{2,1,0:T(8,128)(2,1)S(1)} %copy-done.4), kind=kOutput, calls=%fused_computation.33 | convolution fusion | flops 2148007936 | bytes 7340032 | tf_op jit(solution)/shard_map/rf,df->rd/dot_general | solution.py:63
  81.4 2.3 reshape.70
  85.5 8.6 %all-to-all-start.2 = ((bf16[128,4,1024]{2,1,0:T(4,128)(2,1)}), bf16[128,4,1024]{2,1,0:T(4,128)(2,1)}, u32[]{:S(2)}, u32[]{:S(2)}) async-start(bf16[128,4,1024]{2,1,0:T(4,128)(2,1)} %reshape.70), calls=%async_computation.2 | async-start | bytes 2097152 | tf_op jit(solution)/shard_map/all_to_all | solution.py:40
  94.0 6.5 %convert_bitcast_fusion.1 = bf16[1,1024,2048]{2,1,0:T(8,128)(2,1)} fusion(bf16[512,1024]{1,0:T(8,128)(2,1)} %reshape.69, bf16[512,2048]{1,0:T(8,128)(2,1)} %copy-done.7), kind=kOutput, calls=%fused_computation.26 | convolution fusion | flops 2149580800 | bytes 7340032 | tf_op jit(solution)/shard_map/rd,rf->df/dot_general | solution.py:60
  100.5 5.0 %convert_bitcast_fusion = bf16[1,2048,1024]{2,1,0:T(8,128)(2,1)} fusion(bf16[512,1024]{1,0:T(8,128)(2,1)S(1)} %copy-done.2, f32[512,2048]{1,0:T(8,128)S(1)} %copy-done.6), kind=kOutput, calls=%fused_computation.25 | convolution fusion | flops 2159017984 | bytes 9437184 | tf_op jit(solution)/shard_map/rf,rd->fd/dot_general | solution.py:56
  107.1 5.5 %all-to-all-done.2 = bf16[128,4,1024]{2,1,0:T(4,128)(2,1)} async-done(((bf16[128,4,1024]{2,1,0:T(4,128)(2,1)}), bf16[128,4,1024]{2,1,0:T(4,128)(2,1)}, u32[]{:S(2)}, u32[]{:S(2)}) %all-to-all-start.2) | async-done | bytes 1048608 | tf_op jit(solution)/shard_map/all_to_all | solution.py:40
  115.8 2.2 reshape.72
  119.3 2.0 fusion.32
  122.3 4.6 %all-to-all-start.4 = ((bf16[128,2,1024]{2,1,0:T(2,128)(2,1)}), bf16[128,2,1024]{2,1,0:T(2,128)(2,1)S(1)}, u32[]{:S(2)}, u32[]{:S(2)}) async-start(bf16[128,2,1024]{2,1,0:T(2,128)(2,1)} %reshape.77), calls=%async_computation.4 | async-start | bytes 1048576 | tf_op jit(solution)/shard_map/all_to_all | solution.py:28
  128.8 4.0 %fusion.25 = bf16[2,256,1024]{2,1,0:T(8,128)(2,1)} fusion(f32[2,256,1024,1]{2,1,3,0:T(8,128)} %fusion.68, f32[2,256,256]{1,2,0:T(8,128)S(1)} %fusion.43, f32[2,256,256]{1,2,0:T(8,128)} %get-tuple-element.13, f32[2,256,256]{1,2,0:T(8,128)} %reshape.72, bf16[1024,256]{1,0:T(8,128)(2,1)} %param.6), kind=kOutput, calls=%fused_computation.29 | convolution fusion | flops 270140160 | bytes 5242880 | tf_op jit(solution)/shard_map/ims,ds->imd/dot_general | solution.py:122
  132.7 7.9 %all-to-all-done.4 = bf16[128,2,1024]{2,1,0:T(2,128)(2,1)S(1)} async-done(((bf16[128,2,1024]{2,1,0:T(2,128)(2,1)}), bf16[128,2,1024]{2,1,0:T(2,128)(2,1)S(1)}, u32[]{:S(2)}, u32[]{:S(2)}) %all-to-all-start.4) | async-done | bytes 524320 | tf_op jit(solution)/shard_map/all_to_all | solution.py:28
  141.1 174.2 %all-gather = bf16[128,2,1024]{2,1,0:T(2,128)(2,1)S(1)} all-gather(bf16[1,2,1024]{2,1,0:T(2,128)(2,1)S(1)} %bitcast.108), channel_id=1, replica_groups=mesh['wide'=32,'narrow'=4] {'wide','narrow'}, dimensions={0}, use_global_device_ids=true | all-gather | bytes 528384 | tf_op jit(solution)/shard_map/all_gather | solution.py:129
  (38 shorter events, 25.1 us)
Async XLA Ops:
  0.6 1.2 copy-start
  5.2 17.6 %copy-start.1 = (bf16[512,1024]{1,0:T(8,128)(2,1)S(1)}, bf16[512,1024]{1,0:T(8,128)(2,1)}, u32[]{:S(2)}) copy-start(bf16[512,1024]{1,0:T(8,128)(2,1)} %param.9) | copy-start | bytes 3145732
  6.9 30.4 %all-to-all-start.1 = ((bf16[128,4,1024]{2,1,0:T(4,128)(2,1)}), bf16[128,4,1024]{2,1,0:T(4,128)(2,1)S(1)}, u32[]{:S(2)}, u32[]{:S(2)}) async-start(bf16[128,4,1024]{2,1,0:T(4,128)(2,1)} %copy.34), calls=%async_computation.1 | async-start | bytes 2097152 | tf_op jit(solution)/shard_map/all_to_all | solution.py:28
  37.4 24.4 %all-to-all-start = ((bf16[128,4,1024]{2,1,0:T(4,128)(2,1)}), bf16[128,4,1024]{2,1,0:T(4,128)(2,1)}, u32[]{:S(2)}, u32[]{:S(2)}) async-start(bf16[128,4,1024]{2,1,0:T(4,128)(2,1)} %copy.32), calls=%async_computation | async-start | bytes 2097152 | tf_op jit(solution)/shard_map/all_to_all | solution.py:36
  44.2 7.0 %copy-start.3 = (bf16[1,2048,1024]{2,1,0:T(8,128)(2,1)S(1)}, bf16[1,2048,1024]{2,1,0:T(8,128)(2,1)}, u32[]{:S(2)}) copy-start(bf16[1,2048,1024]{2,1,0:T(8,128)(2,1)} %param.8) | copy-start | bytes 12582916
  49.2 2.0 copy-start.5
  61.8 23.7 %all-to-all-start.3 = ((bf16[128,4,1024]{2,1,0:T(4,128)(2,1)}), bf16[128,4,1024]{2,1,0:T(4,128)(2,1)S(1)}, u32[]{:S(2)}, u32[]{:S(2)}) async-start(bf16[128,4,1024]{2,1,0:T(4,128)(2,1)} %reshape.73), calls=%async_computation.3 | async-start | bytes 2097152 | tf_op jit(solution)/shard_map/all_to_all | solution.py:32
  68.5 9.5 %copy-start.4 = (bf16[1,1024,2048]{2,1,0:T(8,128)(2,1)S(1)}, bf16[1,1024,2048]{2,1,0:T(8,128)(2,1)}, u32[]{:S(2)}) copy-start(bf16[1,1024,2048]{2,1,0:T(8,128)(2,1)} %param.7) | copy-start | bytes 12582916
  76.7 1.4 copy-start.7
  85.5 27.1 %all-to-all-start.2 = ((bf16[128,4,1024]{2,1,0:T(4,128)(2,1)}), bf16[128,4,1024]{2,1,0:T(4,128)(2,1)}, u32[]{:S(2)}, u32[]{:S(2)}) async-start(bf16[128,4,1024]{2,1,0:T(4,128)(2,1)} %reshape.70), calls=%async_computation.2 | async-start | bytes 2097152 | tf_op jit(solution)/shard_map/all_to_all | solution.py:40
  94.0 6.5 %copy-start.2 = (bf16[512,1024]{1,0:T(8,128)(2,1)S(1)}, bf16[512,1024]{1,0:T(8,128)(2,1)}, u32[]{:S(2)}) copy-start(bf16[512,1024]{1,0:T(8,128)(2,1)} %reshape.67) | copy-start | bytes 3145732
  94.0 6.5 %copy-start.6 = (f32[512,2048]{1,0:T(8,128)S(1)}, f32[512,2048]{1,0:T(8,128)}, u32[]{:S(2)}) copy-start(f32[512,2048]{1,0:T(8,128)} %copy-done.5) | copy-start | bytes 12582916
  122.3 18.3 %all-to-all-start.4 = ((bf16[128,2,1024]{2,1,0:T(2,128)(2,1)}), bf16[128,2,1024]{2,1,0:T(2,128)(2,1)S(1)}, u32[]{:S(2)}, u32[]{:S(2)}) async-start(bf16[128,2,1024]{2,1,0:T(2,128)(2,1)} %reshape.77), calls=%async_computation.4 | async-start | bytes 1048576 | tf_op jit(solution)/shard_map/all_to_all | solution.py:28

commit v2 on v0

v2 whole, which is shorter than its diff:
```python
import math

import jax
import jax.numpy as jnp
from jax import lax
from jax.experimental import pallas as pl
from jax.experimental.pallas import tpu as pltpu
from jax.sharding import PartitionSpec as P

MESH = pl.DeviceIdType.MESH
F32 = jnp.float32
BF16 = jnp.bfloat16
N = 128
WIDTH = 1024
FF = 2048
M = 256
SLOTS = 256
ROWS = 8
GROUP = 32
GROUPS = N // GROUP
CHUNK = GROUP * ROWS
HALF = CHUNK // 2
FTILE = 512
STRIDE = 37

root_two_pi = math.sqrt(2.0 / math.pi)
cubic_coef = 0.044715


def dot(a, b, ca=1, cb=0):
    return lax.dot_general(a, b, (((ca,), (cb,)), ((), ())), preferred_element_type=F32)


def kernel(
    tokens_hbm,
    router_hbm,
    first_hbm,
    second_hbm,
    upstream_hbm,
    token_grad_hbm,
    router_grad_hbm,
    first_grad_hbm,
    second_grad_hbm,
    tokens,
    router,
    first,
    second,
    upstream,
    router_rel,
    turn,
    interleave,
    dispatch,
    combine,
    parts,
    send_buf,
    recv_buf,
    rows_in,
    rows_grad,
    active,
    pre_grad,
    out_acc,
    back_acc,
    back_buf,
    return_buf,
    first_grad,
    second_grad,
    token_grad,
    logit_abs,
    terms,
    terms_in,
    own_sum,
    gathered,
    router_grad,
    load_sem,
    store_sem,
    send_sem,
    recv_sem,
    back_send_sem,
    back_recv_sem,
    term_sem,
    gather_sem,
):
    me = lax.axis_index("wide") * 4 + lax.axis_index("narrow")

    def device(number):
        return (number // 4, number % 4)

    def ahead(k):
        return (me + STRIDE * k) % N

    def behind(k):
        return (me + (N - STRIDE) * k) % N

    loads = [
        pltpu.make_async_copy(src, dst, load_sem.at[n])
        for n, (src, dst) in enumerate(
            (
                (router_hbm, router),
                (tokens_hbm, tokens),
                (upstream_hbm, upstream),
                (first_hbm.at[0], first),
                (second_hbm.at[0], second),
            )
        )
    ]
    for load in loads:
        load.start()

    barrier = pltpu.get_barrier_semaphore()

    def greet(k, carry):
        pl.semaphore_signal(barrier, inc=1, device_id=device((me + k) % N), device_id_type=MESH)
        return carry

    lax.fori_loop(1, N, greet, 0)

    row = lax.broadcasted_iota(jnp.int32, (SLOTS, SLOTS), 0)
    col = lax.broadcasted_iota(jnp.int32, (SLOTS, SLOTS), 1)
    slot = 2 * ((me + STRIDE * (col >> 1)) & (N - 1)) + (col & 1)
    turn[...] = jnp.where(row == slot, 1.0, 0.0).astype(BF16)
    row = lax.broadcasted_iota(jnp.int32, (CHUNK, CHUNK), 0)
    col = lax.broadcasted_iota(jnp.int32, (CHUNK, CHUNK), 1)
    origin = ((row >> 1) & 3) * (2 * GROUP) + 2 * (row >> 3) + (row & 1)
    interleave[...] = jnp.where(col == origin, 1.0, 0.0).astype(BF16)

    loads[0].wait()
    router_rel[...] = dot(router[...], turn[...]).astype(BF16)
    loads[1].wait()
    loads[2].wait()
    for i in range(2):
        image = pl.ds(M * i, M)
        logits = dot(tokens[image, :], router_rel[...])
        top = jnp.exp(logits - jnp.max(logits, axis=0, keepdims=True))
        disp = top / jnp.sum(top, axis=0, keepdims=True)
        top = jnp.exp(logits - jnp.max(logits, axis=1, keepdims=True))
        comb = top / jnp.sum(top, axis=1, keepdims=True)
        dispatch[image, :] = disp
        combine[image, :] = comb
        parts[i] = dot(disp.astype(BF16), tokens[image, :], 0, 0).astype(BF16)
        parts[2 + i] = dot(comb.astype(BF16), upstream[image, :], 0, 0).astype(BF16)

    pl.semaphore_wait(barrier, N - 1)

    def send_copy(k):
        return pltpu.make_async_remote_copy(
            src_ref=send_buf.at[k],
            dst_ref=recv_buf.at[k],
            send_sem=send_sem,
            recv_sem=recv_sem.at[k // GROUP],
            device_id=device(ahead(k)),
            device_id_type=MESH,
        )

    own = pltpu.make_async_copy(send_buf.at[0], recv_buf.at[0], recv_sem.at[0])
    for g in range(GROUPS):
        stack = parts[:, 2 * GROUP * g : 2 * GROUP * (g + 1), :].reshape(CHUNK, WIDTH)
        send_buf[GROUP * g : GROUP * (g + 1)] = (
            dot(interleave[...], stack).astype(BF16).reshape(GROUP, ROWS, WIDTH)
        )
        if g == 0:
            own.start()

        def send(k, carry):
            send_copy(k).start()
            return carry

        lax.fori_loop(max(1, GROUP * g), GROUP * (g + 1), send, 0)

    loads[3].wait()
    loads[4].wait()

    def back_copy(k):
        return pltpu.make_async_remote_copy(
            src_ref=back_buf.at[k],
            dst_ref=return_buf.at[k],
            send_sem=back_send_sem,
            recv_sem=back_recv_sem,
            device_id=device(behind(k)),
            device_id_type=MESH,
        )

    def expert(g, carry):
        group = pl.ds(pl.multiple_of(g * GROUP, GROUP), GROUP)
        rows = pl.ds(pl.multiple_of(g * HALF, HALF), HALF)
        pltpu.make_async_copy(recv_buf.at[group], recv_buf.at[group], recv_sem.at[g]).wait()
        split = dot(interleave[...], recv_buf[group].reshape(CHUNK, WIDTH), 0, 0).astype(BF16)
        rows_in[rows, :] = split[:HALF]
        rows_grad[rows, :] = split[HALF:]
        out_acc[...] = jnp.zeros_like(out_acc)
        back_acc[...] = jnp.zeros_like(back_acc)

        def tile(t, inner):
            cols = pl.ds(pl.multiple_of(t * FTILE, FTILE), FTILE)
            hidden = dot(rows_in[rows, :], first[:, cols])
            grad = dot(rows_grad[rows, :], second[cols, :], 1, 1)
            square = hidden * hidden
            tangent = jnp.tanh(root_two_pi * (hidden + cubic_coef * square * hidden))
            act = (0.5 * hidden * (1.0 + tangent)).astype(BF16)
            slope = 0.5 * (1.0 + tangent) + 0.5 * hidden * (1.0 - tangent * tangent) * root_two_pi * (
                1.0 + 3.0 * cubic_coef * square
            )
            pre = (grad * slope).astype(BF16)
            active[rows, cols] = act
            pre_grad[rows, cols] = pre
            out_acc[...] += dot(act, second[cols, :])
            back_acc[...] += dot(pre, first[:, cols], 1, 1)
            return inner

        lax.fori_loop(0, FF // FTILE, tile, 0)
        both = jnp.concatenate([out_acc[...].astype(BF16), back_acc[...].astype(BF16)], axis=0)
        back_buf[group] = dot(interleave[...], both).astype(BF16).reshape(GROUP, ROWS, WIDTH)

        @pl.when(g == 0)
        def _():
            pltpu.make_async_copy(back_buf.at[0], return_buf.at[0], back_recv_sem).start()

        def send(k, inner):
            back_copy(k).start()
            return inner

        lax.fori_loop(jnp.maximum(1, GROUP * g), GROUP * (g + 1), send, 0)
        return carry

    lax.fori_loop(0, GROUPS, expert, 0)

    def weights(t, carry):
        cols = pl.ds(pl.multiple_of(t * FTILE, FTILE), FTILE)
        second_grad[cols, :] = dot(active[:, cols], rows_grad[...], 0, 0).astype(BF16)
        first_grad[:, cols] = dot(rows_in[...], pre_grad[:, cols], 0, 0).astype(BF16)
        return carry

    lax.fori_loop(0, FF // FTILE, weights, 0)
    stores = [
        pltpu.make_async_copy(src, dst, store_sem.at[n])
        for n, (src, dst) in enumerate(
            (
                (first_grad, first_grad_hbm.at[0]),
                (second_grad, second_grad_hbm.at[0]),
                (token_grad, token_grad_hbm),
                (router_grad, router_grad_hbm),
            )
        )
    ]
    stores[0].start()
    stores[1].start()

    pltpu.make_async_copy(return_buf, return_buf, back_recv_sem).wait()
    for g in range(GROUPS):
        chunk = return_buf[GROUP * g : GROUP * (g + 1)].reshape(CHUNK, WIDTH)
        split = dot(interleave[...], chunk, 0, 0).astype(BF16)
        parts[:, 2 * GROUP * g : 2 * GROUP * (g + 1), :] = split.reshape(4, 2 * GROUP, WIDTH)
    lows = []
    for i in range(2):
        image = pl.ds(M * i, M)
        disp = dispatch[image, :]
        comb = combine[image, :]
        combine_grad = dot(upstream[image, :], parts[i], 1, 1)
        dispatch_grad = dot(tokens[image, :], parts[2 + i], 1, 1)
        logit_grad = disp * (dispatch_grad - jnp.sum(disp * dispatch_grad, axis=0, keepdims=True))
        logit_grad = logit_grad + comb * (
            combine_grad - jnp.sum(comb * combine_grad, axis=1, keepdims=True)
        )
        low = logit_grad.astype(BF16)
        lows.append(low)
        logit_abs[image, :] = dot(low, turn[...], 1, 1).astype(BF16)
    total = dot(tokens[...], logit_abs[...], 0, 0).astype(BF16)
    terms[0] = total[:, :128]
    terms[1] = total[:, 128:]

    def block(ref, number):
        return ref.at[number % 2, pl.ds(pl.multiple_of((number // 2) * 16, 16), 16), :]

    pltpu.make_async_copy(block(terms, me), terms_in.at[0], term_sem.at[1]).start()

    def send_term(k, carry):
        pltpu.make_async_remote_copy(
            src_ref=block(terms, ahead(k)),
            dst_ref=terms_in.at[k],
            send_sem=term_sem.at[0],
            recv_sem=term_sem.at[1],
            device_id=device(ahead(k)),
            device_id_type=MESH,
        ).start()
        return carry

    lax.fori_loop(1, N, send_term, 0)

    for i in range(2):
        image = pl.ds(M * i, M)
        token_grad[image, :] = (
            dot(dispatch[image, :].astype(BF16), parts[2 + i]) + dot(lows[i], router_rel[...], 1, 1)
        ).astype(BF16)
    stores[2].start()

    pltpu.make_async_copy(terms_in, terms_in, term_sem.at[1]).wait()
    own_sum[...] = jnp.sum(terms_in[...].astype(F32), axis=0).astype(BF16)
    pltpu.make_async_copy(own_sum, block(gathered, me), gather_sem.at[1]).start()

    def send_sum(k, carry):
        pltpu.make_async_remote_copy(
            src_ref=own_sum,
            dst_ref=block(gathered, me),
            send_sem=gather_sem.at[0],
            recv_sem=gather_sem.at[1],
            device_id=device(ahead(k)),
            device_id_type=MESH,
        ).start()
        return carry

    lax.fori_loop(1, N, send_sum, 0)
    pltpu.make_async_copy(gathered, gathered, gather_sem.at[1]).wait()
    router_grad[:, :128] = gathered[0].astype(F32)
    router_grad[:, 128:] = gathered[1].astype(F32)
    stores[3].start()

    most = pl.ds(1, N - 1)
    pltpu.make_async_copy(send_buf.at[most], send_buf.at[most], send_sem).wait()
    pltpu.make_async_copy(back_buf.at[most], back_buf.at[most], back_send_sem).wait()
    pltpu.make_async_copy(terms_in.at[most], terms_in.at[most], term_sem.at[0]).wait()
    pltpu.make_async_copy(terms_in.at[most], terms_in.at[most], gather_sem.at[0]).wait()
    for store in stores:
        store.wait()


def local(tokens, router, expert_in, expert_out, upstream):
    hbm = pl.BlockSpec(memory_space=pl.ANY)
    vmem = pltpu.VMEM
    dma = pltpu.SemaphoreType.DMA
    token_grad, router_grad, first_grad, second_grad = pl.pallas_call(
        kernel,
        out_shape=(
            jax.ShapeDtypeStruct((2 * M, WIDTH), BF16),
            jax.ShapeDtypeStruct((WIDTH, SLOTS), F32),
            jax.ShapeDtypeStruct((1, WIDTH, FF), BF16),
            jax.ShapeDtypeStruct((1, FF, WIDTH), BF16),
        ),
        in_specs=[hbm] * 5,
        out_specs=(hbm,) * 4,
        scratch_shapes=[
            vmem((2 * M, WIDTH), BF16),
            vmem((WIDTH, SLOTS), BF16),
            vmem((WIDTH, FF), BF16),
            vmem((FF, WIDTH), BF16),
            vmem((2 * M, WIDTH), BF16),
            vmem((WIDTH, SLOTS), BF16),
            vmem((SLOTS, SLOTS), BF16),
            vmem((CHUNK, CHUNK), BF16),
            vmem((2 * M, SLOTS), F32),
            vmem((2 * M, SLOTS), F32),
            vmem((4, SLOTS, WIDTH), BF16),
            vmem((N, ROWS, WIDTH), BF16),
            vmem((N, ROWS, WIDTH), BF16),
            vmem((4 * N, WIDTH), BF16),
            vmem((4 * N, WIDTH), BF16),
            vmem((4 * N, FF), BF16),
            vmem((4 * N, FF), BF16),
            vmem((HALF, WIDTH), F32),
            vmem((HALF, WIDTH), F32),
            vmem((N, ROWS, WIDTH), BF16),
            vmem((N, ROWS, WIDTH), BF16),
            vmem((WIDTH, FF), BF16),
            vmem((FF, WIDTH), BF16),
            vmem((2 * M, WIDTH), BF16),
            vmem((2 * M, SLOTS), BF16),
            vmem((2, WIDTH, 128), BF16),
            vmem((N, 16, 128), BF16),
            vmem((16, 128), BF16),
            vmem((2, WIDTH, 128), BF16),
            vmem((WIDTH, SLOTS), F32),
            dma((5,)),
            dma((4,)),
            dma,
            dma((GROUPS,)),
            dma,
            dma,
            dma((2,)),
            dma((2,)),
        ],
        compiler_params=pltpu.CompilerParams(
            collective_id=0, has_side_effects=True, vmem_limit_bytes=56 << 20
        ),
        cost_estimate=pl.CostEstimate(flops=16 * 10**9, bytes_accessed=24 * 10**6, transcendentals=2 * 10**6),
    )(tokens, router, expert_in, expert_out, upstream)
    return (token_grad, router_grad, first_grad, second_grad)


def solution(mesh):
    return jax.shard_map(
        local,
        mesh=mesh,
        in_specs=(
            P(("wide", "narrow"), None),
            P(),
            P(("wide", "narrow"), None, None),
            P(("wide", "narrow"), None, None),
            P(("wide", "narrow"), None),
        ),
        out_specs=(
            P(("wide", "narrow"), None),
            P(),
            P(("wide", "narrow"), None, None),
            P(("wide", "narrow"), None, None),
        ),
        check_vma=False,
    )
```

time: 281 us -> 96.1 us (0.34)
  waiting for transfers between devices: 163 us -> 0 us
  Pallas kernels: 0 us -> 84.9 us
  matrix products: 47.1 us -> 0 us
  starting transfers between devices: 30.6 us -> 0 us
  between operations: 14.2 us -> 0.65 us
  local copies, waits for them, and re-layouts: 23.6 us -> 10.4 us
    psum x1 -> x0, waiting for transfers between devices: 138 us -> none  [local(): router_grad = lax.psum(router_part, ('wide', 'narrow'))]
    pallas_call x0 -> x1, Pallas kernels: none -> 84.9 us  [local(): pl.pallas_call(kernel, out_shape=(jax.ShapeDtypeStruct((2 * M, WIDTH), BF...]
    dot_general x13 -> x0, matrix products: 42 us -> none  [the longest x1 8.14 us: expert_backward(): jnp.einsum('rd,fd->rf', rows_grad, second_weight, preferred_element_type=...]
    all_to_all x4 -> x0, starting transfers between devices: 30.3 us -> none  [the longest x1 11.5 us: send_inputs(): lax.all_to_all(array, ('wide', 'narrow'), split_axis=0, concat_axis=0, ti...]
    all_to_all x4 -> x0, waiting for transfers between devices: 25.2 us -> none  [the longest x1 11.4 us: send_inputs(): lax.all_to_all(array, ('wide', 'narrow'), split_axis=0, concat_axis=0, ti...]
    reshape x11 -> x0, local copies, waits for them, and re-layouts: 13.8 us -> none  [the longest x1 2.26 us: local(): slot_return = send_returns(slot_back.reshape(slot_shape))]
    div x2 -> x0, matrix products: 5.06 us -> none  [the longest x1 2.56 us: local(): combine = jax.nn.softmax(logits, axis=2)]
    unnamed x19 -> x8, local copies, waits for them, and re-layouts: 7.14 us -> 10.4 us
  transfers between devices with their start and end apart: 5 -> 0, of which waited for: 5 -> 0; matrix products, arithmetic and copies ran while one was open for 19% -> 0% of each run, Pallas kernels for 0% -> 0%
where the time goes in v2:
time: 96.1 us; the launch traced here: 95.9 us
  Pallas kernels  84.9 us (88%)
  local copies, waits for them, and re-layouts  10.4 us (11%)
    pallas_call x1, Pallas kernels, local(): pl.pallas_call(kernel, out_shape=(jax.ShapeDtypeStruct((2 * M, WIDTH), BF...  84.9 us
    unnamed x8, local copies, waits for them, and re-layouts  10.4 us

profile of v2, /device:TPU:1, one launch (start us, length us, event | category | flops | bytes accessed | tf_op | source)
XLA Modules:
  0.0 95.9 jit_solution(247903838676685510)
XLA Ops:
  0.6 84.9 %shard_map.84 = (bf16[512,1024]{1,0:T(8,128)(2,1)}, f32[1024,256]{1,0:T(8,128)}, bf16[1,1024,2048]{2,1,0:T(8,128)(2,1)}, bf16[1,2048,1024]{2,1,0:T(8,128)(2,1)}) custom-call(bf16[512,1024]{1,0:T(8,128)(2,1)} %tokens_hbm.1, bf16[1024,256]{1,0:T(8,128)(2,1)} %router_hbm.1, bf16[1,1024,2048]{2,1,0:T(8,128)(2,1)} %first_hbm.1, ...), custom_call_target="tpu_custom_call" | custom-call | flops 16000000000 | bytes 24000000 | tf_op jit(solution)/shard_map/pallas_call | solution.py:329
  85.5 0.0 copy-start.1
  85.5 2.4 %copy.13 = bf16[512,1024]{1,0:T(8,128)(2,1)} copy(bf16[512,1024]{1,0:T(8,128)(2,1)} %get-tuple-element.8) | data formatting | bytes 2097152
  87.9 2.3 %copy.14 = f32[1024,256]{1,0:T(8,128)} copy(f32[1024,256]{1,0:T(8,128)} %get-tuple-element.9) | data formatting | bytes 2097152
  90.2 0.0 copy-done.1
  90.2 0.0 copy-start
  90.2 2.1 %copy.15 = bf16[1,1024,2048]{2,1,0:T(8,128)(2,1)} copy(bf16[1,1024,2048]{2,1,0:T(8,128)(2,1)S(1)} %copy-done.1) | data formatting | bytes 8388608
  92.4 1.6 %copy-done = bf16[1,2048,1024]{2,1,0:T(8,128)(2,1)S(1)} copy-done((bf16[1,2048,1024]{2,1,0:T(8,128)(2,1)S(1)}, bf16[1,2048,1024]{2,1,0:T(8,128)(2,1)}, u32[]{:S(2)}) %copy-start) | copy-done | bytes 4194328
  93.9 2.0 %copy.16 = bf16[1,2048,1024]{2,1,0:T(8,128)(2,1)} copy(bf16[1,2048,1024]{2,1,0:T(8,128)(2,1)S(1)} %copy-done) | data formatting | bytes 8388608
Async XLA Ops:
  85.5 4.7 %copy-start.1 = (bf16[1,1024,2048]{2,1,0:T(8,128)(2,1)S(1)}, bf16[1,1024,2048]{2,1,0:T(8,128)(2,1)}, u32[]{:S(2)}) copy-start(bf16[1,1024,2048]{2,1,0:T(8,128)(2,1)} %get-tuple-element.10) | copy-start | bytes 12582916
  90.2 3.7 %copy-start = (bf16[1,2048,1024]{2,1,0:T(8,128)(2,1)S(1)}, bf16[1,2048,1024]{2,1,0:T(8,128)(2,1)}, u32[]{:S(2)}) copy-start(bf16[1,2048,1024]{2,1,0:T(8,128)(2,1)} %get-tuple-element.11) | copy-start | bytes 12582916

commit v3 on v2

--- a/solution.py
+++ b/solution.py
@@ -18,6 +18,9 @@
 ROWS = 8
 GROUP = 32
 GROUPS = N // GROUP
+CHIPS = N // 2
+NEAR = 16
+FAR = N // NEAR - 1
 CHUNK = GROUP * ROWS
 HALF = CHUNK // 2
 FTILE = 512
@@ -37,10 +40,10 @@
     first_hbm,
     second_hbm,
     upstream_hbm,
-    token_grad_hbm,
-    router_grad_hbm,
-    first_grad_hbm,
-    second_grad_hbm,
+    token_grad,
+    router_grad,
+    first_grad,
+    second_grad,
     tokens,
     router,
     first,
@@ -62,23 +65,23 @@
     back_acc,
     back_buf,
     return_buf,
-    first_grad,
-    second_grad,
-    token_grad,
     logit_abs,
     terms,
+    pair_in,
+    chip_sum,
     terms_in,
     own_sum,
     gathered,
-    router_grad,
     load_sem,
-    store_sem,
     send_sem,
     recv_sem,
     back_send_sem,
     back_recv_sem,
     term_sem,
     gather_sem,
+    pair_sem,
+    whole_sem,
+    round_sem,
 ):
     me = lax.axis_index("wide") * 4 + lax.axis_index("narrow")
 
@@ -140,7 +143,6 @@
         parts[2 + i] = dot(comb.astype(BF16), upstream[image, :], 0, 0).astype(BF16)
 
     pl.semaphore_wait(barrier, N - 1)
-
     def send_copy(k):
         return pltpu.make_async_remote_copy(
             src_ref=send_buf.at[k],
@@ -164,7 +166,11 @@
             send_copy(k).start()
             return carry
 
-        lax.fori_loop(max(1, GROUP * g), GROUP * (g + 1), send, 0)
+        if g == 0:
+            lax.fori_loop(1, NEAR, send, 0)
+            lax.fori_loop(NEAR, GROUP, send, 0)
+        else:
+            lax.fori_loop(GROUP * g, GROUP * (g + 1), send, 0)
 
     loads[3].wait()
     loads[4].wait()
@@ -225,25 +231,11 @@
 
     def weights(t, carry):
         cols = pl.ds(pl.multiple_of(t * FTILE, FTILE), FTILE)
-        second_grad[cols, :] = dot(active[:, cols], rows_grad[...], 0, 0).astype(BF16)
-        first_grad[:, cols] = dot(rows_in[...], pre_grad[:, cols], 0, 0).astype(BF16)
+        second_grad[0, cols, :] = dot(active[:, cols], rows_grad[...], 0, 0).astype(BF16)
+        first_grad[0, :, cols] = dot(rows_in[...], pre_grad[:, cols], 0, 0).astype(BF16)
         return carry
 
     lax.fori_loop(0, FF // FTILE, weights, 0)
-    stores = [
-        pltpu.make_async_copy(src, dst, store_sem.at[n])
-        for n, (src, dst) in enumerate(
-            (
-                (first_grad, first_grad_hbm.at[0]),
-                (second_grad, second_grad_hbm.at[0]),
-                (token_grad, token_grad_hbm),
-                (router_grad, router_grad_hbm),
-            )
-        )
-    ]
-    stores[0].start()
-    stores[1].start()
-
     pltpu.make_async_copy(return_buf, return_buf, back_recv_sem).wait()
     for g in range(GROUPS):
         chunk = return_buf[GROUP * g : GROUP * (g + 1)].reshape(CHUNK, WIDTH)
@@ -267,75 +259,106 @@
     terms[0] = total[:, :128]
     terms[1] = total[:, 128:]
 
-    def block(ref, number):
-        return ref.at[number % 2, pl.ds(pl.multiple_of((number // 2) * 16, 16), 16), :]
-
-    pltpu.make_async_copy(block(terms, me), terms_in.at[0], term_sem.at[1]).start()
-
-    def send_term(k, carry):
+    core = me % 2
+    partner = device(me + 1 - 2 * core)
+
+    pair = pltpu.make_async_remote_copy(
+        src_ref=terms.at[1 - core],
+        dst_ref=pair_in,
+        send_sem=pair_sem.at[0],
+        recv_sem=pair_sem.at[1],
+        device_id=partner,
+        device_id_type=MESH,
+    )
+    pair.start()
+    pair.wait_recv()
+    chip_sum[...] = (
+        (terms[core].astype(F32) + pair_in[...].astype(F32)).astype(BF16).reshape(CHIPS, 16, 128)
+    )
+    pltpu.make_async_copy(chip_sum.at[me // 2], terms_in.at[0], term_sem.at[1]).start()
+
+    def send_term(j, carry):
         pltpu.make_async_remote_copy(
-            src_ref=block(terms, ahead(k)),
-            dst_ref=terms_in.at[k],
+            src_ref=chip_sum.at[ahead(2 * j) // 2],
+            dst_ref=terms_in.at[j],
             send_sem=term_sem.at[0],
             recv_sem=term_sem.at[1],
-            device_id=device(ahead(k)),
+            device_id=device(ahead(2 * j)),
             device_id_type=MESH,
         ).start()
         return carry
 
-    lax.fori_loop(1, N, send_term, 0)
+    lax.fori_loop(1, CHIPS, send_term, 0)
 
     for i in range(2):
         image = pl.ds(M * i, M)
         token_grad[image, :] = (
             dot(dispatch[image, :].astype(BF16), parts[2 + i]) + dot(lows[i], router_rel[...], 1, 1)
         ).astype(BF16)
-    stores[2].start()
 
     pltpu.make_async_copy(terms_in, terms_in, term_sem.at[1]).wait()
     own_sum[...] = jnp.sum(terms_in[...].astype(F32), axis=0).astype(BF16)
-    pltpu.make_async_copy(own_sum, block(gathered, me), gather_sem.at[1]).start()
-
-    def send_sum(k, carry):
+    pltpu.make_async_copy(own_sum, gathered.at[core, me // 2], gather_sem.at[1]).start()
+
+    def send_sum(j, carry):
         pltpu.make_async_remote_copy(
             src_ref=own_sum,
-            dst_ref=block(gathered, me),
+            dst_ref=gathered.at[core, me // 2],
             send_sem=gather_sem.at[0],
             recv_sem=gather_sem.at[1],
-            device_id=device(ahead(k)),
+            device_id=device(ahead(2 * j)),
             device_id_type=MESH,
         ).start()
         return carry
 
-    lax.fori_loop(1, N, send_sum, 0)
-    pltpu.make_async_copy(gathered, gathered, gather_sem.at[1]).wait()
-    router_grad[:, :128] = gathered[0].astype(F32)
-    router_grad[:, 128:] = gathered[1].astype(F32)
-    stores[3].start()
+    lax.fori_loop(1, CHIPS, send_sum, 0)
+    pltpu.make_async_copy(gathered.at[core], gathered.at[core], gather_sem.at[1]).wait()
+    whole = pltpu.make_async_remote_copy(
+        src_ref=gathered.at[core],
+        dst_ref=gathered.at[core],
+        send_sem=whole_sem.at[0],
+        recv_sem=whole_sem.at[1],
+        device_id=partner,
+        device_id_type=MESH,
+    )
+    whole.start()
+    whole.wait()
+    pair.wait_send()
+    router_grad[:, :128] = gathered[0].reshape(WIDTH, 128).astype(F32)
+    router_grad[:, 128:] = gathered[1].reshape(WIDTH, 128).astype(F32)
 
     most = pl.ds(1, N - 1)
     pltpu.make_async_copy(send_buf.at[most], send_buf.at[most], send_sem).wait()
     pltpu.make_async_copy(back_buf.at[most], back_buf.at[most], back_send_sem).wait()
+    most = pl.ds(1, CHIPS - 1)
     pltpu.make_async_copy(terms_in.at[most], terms_in.at[most], term_sem.at[0]).wait()
     pltpu.make_async_copy(terms_in.at[most], terms_in.at[most], gather_sem.at[0]).wait()
-    for store in stores:
-        store.wait()
+
+
+def store_kernel(*refs):
+    ins, outs, sem = refs[:4], refs[4:8], refs[8]
+    copies = [pltpu.make_async_copy(ins[n], outs[n], sem.at[n]) for n in range(4)]
+    for copy in copies:
+        copy.start()
+    for copy in copies:
+        copy.wait()
 
 
 def local(tokens, router, expert_in, expert_out, upstream):
     hbm = pl.BlockSpec(memory_space=pl.ANY)
     vmem = pltpu.VMEM
     dma = pltpu.SemaphoreType.DMA
-    token_grad, router_grad, first_grad, second_grad = pl.pallas_call(
+    shapes = (
+        ((2 * M, WIDTH), BF16),
+        ((WIDTH, SLOTS), F32),
+        ((1, WIDTH, FF), BF16),
+        ((1, FF, WIDTH), BF16),
+    )
+    outs = pl.pallas_call(
         kernel,
-        out_shape=(
-            jax.ShapeDtypeStruct((2 * M, WIDTH), BF16),
-            jax.ShapeDtypeStruct((WIDTH, SLOTS), F32),
-            jax.ShapeDtypeStruct((1, WIDTH, FF), BF16),
-            jax.ShapeDtypeStruct((1, FF, WIDTH), BF16),
-        ),
-        in_specs=[hbm] * 5,
-        out_specs=(hbm,) * 4,
+        out_shape=tuple(vmem(*shape) for shape in shapes),
+        in_specs=[pl.BlockSpec(memory_space=pltpu.HBM)] * 5,
+        out_specs=(pl.BlockSpec(memory_space=vmem),) * 4,
         scratch_shapes=[
             vmem((2 * M, WIDTH), BF16),
             vmem((WIDTH, SLOTS), BF16),
@@ -358,30 +381,40 @@
             vmem((HALF, WIDTH), F32),
             vmem((N, ROWS, WIDTH), BF16),
             vmem((N, ROWS, WIDTH), BF16),
-            vmem((WIDTH, FF), BF16),
-            vmem((FF, WIDTH), BF16),
-            vmem((2 * M, WIDTH), BF16),
             vmem((2 * M, SLOTS), BF16),
             vmem((2, WIDTH, 128), BF16),
-            vmem((N, 16, 128), BF16),
+            vmem((WIDTH, 128), BF16),
+            vmem((CHIPS, 16, 128), BF16),
+            vmem((CHIPS, 16, 128), BF16),
             vmem((16, 128), BF16),
-            vmem((2, WIDTH, 128), BF16),
-            vmem((WIDTH, SLOTS), F32),
+            vmem((2, CHIPS, 16, 128), BF16),
             dma((5,)),
-            dma((4,)),
             dma,
             dma((GROUPS,)),
             dma,
             dma,
             dma((2,)),
             dma((2,)),
+            dma((2,)),
+            dma((2,)),
+            pltpu.SemaphoreType.REGULAR,
         ],
         compiler_params=pltpu.CompilerParams(
-            collective_id=0, has_side_effects=True, vmem_limit_bytes=56 << 20
+            collective_id=0, has_side_effects=True, vmem_limit_bytes=50 << 20
         ),
-        cost_estimate=pl.CostEstimate(flops=16 * 10**9, bytes_accessed=24 * 10**6, transcendentals=2 * 10**6),
+        cost_estimate=pl.CostEstimate(
+            flops=16 * 10**9, bytes_accessed=12 * 10**6, transcendentals=2 * 10**6
+        ),
     )(tokens, router, expert_in, expert_out, upstream)
-    return (token_grad, router_grad, first_grad, second_grad)
+    return pl.pallas_call(
+        store_kernel,
+        out_shape=tuple(jax.ShapeDtypeStruct(*shape) for shape in shapes),
+        in_specs=[pl.BlockSpec(memory_space=vmem)] * 4,
+        out_specs=(hbm,) * 4,
+        scratch_shapes=[dma((4,))],
+        compiler_params=pltpu.CompilerParams(vmem_limit_bytes=16 << 20),
+        cost_estimate=pl.CostEstimate(flops=0, bytes_accessed=10 * 10**6, transcendentals=0),
+    )(*outs)
 
 
 def solution(mesh):

time: 96.1 us -> 86.6 us (0.901)
  local copies, waits for them, and re-layouts: 10.4 us -> 0 us
  Pallas kernels: 84.9 us -> 85.9 us
    unnamed x8 -> x0, local copies, waits for them, and re-layouts: 10.4 us -> none
    pallas_call x1 -> x2, Pallas kernels: 84.9 us -> 85.9 us  [the longest x1 81.8 us: local(): pl.pallas_call(kernel, out_shape=tuple((vmem(*shape) for shape in shapes)...]
where the time goes in v3:
time: 86.6 us; the launch traced here: 86.5 us
  Pallas kernels  85.9 us (99%)
    pallas_call x1, Pallas kernels, local(): pl.pallas_call(kernel, out_shape=tuple((vmem(*shape) for shape in shapes)...  81.8 us
    pallas_call x1, Pallas kernels, local(): pl.pallas_call(store_kernel, out_shape=tuple((jax.ShapeDtypeStruct(*shape...  4.12 us

profile of v3, /device:TPU:1, one launch (start us, length us, event | category | flops | bytes accessed | tf_op | source)
XLA Modules:
  0.0 86.5 jit_solution(1587795233107674721)
XLA Ops:
  0.6 81.8 %shard_map.84 = (bf16[512,1024]{1,0:T(8,128)(2,1)S(1)}, f32[1024,256]{1,0:T(8,128)S(1)}, bf16[1,1024,2048]{2,1,0:T(8,128)(2,1)S(1)}, bf16[1,2048,1024]{2,1,0:T(8,128)(2,1)S(1)}) custom-call(bf16[512,1024]{1,0:T(8,128)(2,1)} %tokens_hbm.1, bf16[1024,256]{1,0:T(8,128)(2,1)} %router_hbm.1, bf16[1,1024,2048]{2,1,0:T(8,128)(2,1)} %first_hbm.1, ...), custom_call_target="tpu_custom_call" | custom-call | flops 16000000000 | bytes 12000000 | tf_op jit(solution)/shard_map/pallas_call | solution.py:357
  82.4 4.1 %shard_map.85 = (bf16[512,1024]{1,0:T(8,128)(2,1)}, f32[1024,256]{1,0:T(8,128)}, bf16[1,1024,2048]{2,1,0:T(8,128)(2,1)}, bf16[1,2048,1024]{2,1,0:T(8,128)(2,1)}) custom-call(bf16[512,1024]{1,0:T(8,128)(2,1)S(1)} %get-tuple-element.8.refs_0_, f32[1024,256]{1,0:T(8,128)S(1)} %get-tuple-element.9.refs_1_, bf16[1,1024,2048]{2,1,0:T(8,128)(2,1)S(1)} %get-tuple-element.10.refs_2_, ...), custom_call_target="tpu_custom_call" | custom-call | bytes 10000000 | tf_op jit(solution)/shard_map/pallas_call | solution.py:409

commit v4 on v3

--- a/solution.py
+++ b/solution.py
@@ -52,6 +52,7 @@
     router_rel,
     turn,
     interleave,
+    separate,
     dispatch,
     combine,
     parts,
@@ -65,6 +66,10 @@
     back_acc,
     back_buf,
     return_buf,
+    upright,
+    router_flat,
+    flipped,
+    grads,
     logit_abs,
     terms,
     pair_in,
@@ -106,16 +111,20 @@
             )
         )
     ]
-    for load in loads:
+
+    barrier = pltpu.get_barrier_semaphore()
+
+    def greet(k, carry):
+        pl.semaphore_signal(barrier, inc=1, device_id=device(behind(k)), device_id_type=MESH)
+        return carry
+
+    def greet_far(k, carry):
+        return greet(NEAR * k, carry)
+
+    lax.fori_loop(1, NEAR, greet, 0)
+    lax.fori_loop(1, FAR + 1, greet_far, 0)
+    for load in loads[:3]:
         load.start()
-
-    barrier = pltpu.get_barrier_semaphore()
-
-    def greet(k, carry):
-        pl.semaphore_signal(barrier, inc=1, device_id=device((me + k) % N), device_id_type=MESH)
-        return carry
-
-    lax.fori_loop(1, N, greet, 0)
 
     row = lax.broadcasted_iota(jnp.int32, (SLOTS, SLOTS), 0)
     col = lax.broadcasted_iota(jnp.int32, (SLOTS, SLOTS), 1)
@@ -125,11 +134,25 @@
     col = lax.broadcasted_iota(jnp.int32, (CHUNK, CHUNK), 1)
     origin = ((row >> 1) & 3) * (2 * GROUP) + 2 * (row >> 3) + (row & 1)
     interleave[...] = jnp.where(col == origin, 1.0, 0.0).astype(BF16)
+    origin = ((col >> 1) & 3) * (2 * GROUP) + 2 * (col >> 3) + (col & 1)
+    separate[...] = jnp.where(row == origin, 1.0, 0.0).astype(BF16)
 
     loads[0].wait()
     router_rel[...] = dot(router[...], turn[...]).astype(BF16)
+    pl.semaphore_wait(barrier, NEAR - 1 + FAR)
+
+    def tell(k, carry):
+        pl.semaphore_signal(
+            round_sem, inc=1, device_id=device(behind(NEAR * k)), device_id_type=MESH
+        )
+        return carry
+
+    lax.fori_loop(1, FAR + 1, tell, 0)
     loads[1].wait()
     loads[2].wait()
+    loads[3].start()
+    loads[4].start()
+    lows = []
     for i in range(2):
         image = pl.ds(M * i, M)
         logits = dot(tokens[image, :], router_rel[...])
@@ -139,10 +162,8 @@
         comb = top / jnp.sum(top, axis=1, keepdims=True)
         dispatch[image, :] = disp
         combine[image, :] = comb
-        parts[i] = dot(disp.astype(BF16), tokens[image, :], 0, 0).astype(BF16)
-        parts[2 + i] = dot(comb.astype(BF16), upstream[image, :], 0, 0).astype(BF16)
-
-    pl.semaphore_wait(barrier, N - 1)
+        lows.append((disp.astype(BF16), comb.astype(BF16)))
+
     def send_copy(k):
         return pltpu.make_async_remote_copy(
             src_ref=send_buf.at[k],
@@ -155,12 +176,21 @@
 
     own = pltpu.make_async_copy(send_buf.at[0], recv_buf.at[0], recv_sem.at[0])
     for g in range(GROUPS):
+        if g % 2 == 0:
+            slots = slice(2 * GROUP * g, 2 * GROUP * (g + 2))
+            for i in range(2):
+                image = pl.ds(M * i, M)
+                parts[i, slots, :] = dot(lows[i][0][:, slots], tokens[image, :], 0, 0).astype(BF16)
+                parts[2 + i, slots, :] = dot(lows[i][1][:, slots], upstream[image, :], 0, 0).astype(
+                    BF16
+                )
         stack = parts[:, 2 * GROUP * g : 2 * GROUP * (g + 1), :].reshape(CHUNK, WIDTH)
         send_buf[GROUP * g : GROUP * (g + 1)] = (
             dot(interleave[...], stack).astype(BF16).reshape(GROUP, ROWS, WIDTH)
         )
         if g == 0:
             own.start()
+            pl.semaphore_wait(round_sem, FAR)
 
         def send(k, carry):
             send_copy(k).start()
@@ -180,7 +210,7 @@
             src_ref=back_buf.at[k],
             dst_ref=return_buf.at[k],
             send_sem=back_send_sem,
-            recv_sem=back_recv_sem,
+            recv_sem=back_recv_sem.at[k // GROUP],
             device_id=device(behind(k)),
             device_id_type=MESH,
         )
@@ -189,7 +219,7 @@
         group = pl.ds(pl.multiple_of(g * GROUP, GROUP), GROUP)
         rows = pl.ds(pl.multiple_of(g * HALF, HALF), HALF)
         pltpu.make_async_copy(recv_buf.at[group], recv_buf.at[group], recv_sem.at[g]).wait()
-        split = dot(interleave[...], recv_buf[group].reshape(CHUNK, WIDTH), 0, 0).astype(BF16)
+        split = dot(separate[...], recv_buf[group].reshape(CHUNK, WIDTH)).astype(BF16)
         rows_in[rows, :] = split[:HALF]
         rows_grad[rows, :] = split[HALF:]
         out_acc[...] = jnp.zeros_like(out_acc)
@@ -218,7 +248,7 @@
 
         @pl.when(g == 0)
         def _():
-            pltpu.make_async_copy(back_buf.at[0], return_buf.at[0], back_recv_sem).start()
+            pltpu.make_async_copy(back_buf.at[0], return_buf.at[0], back_recv_sem.at[0]).start()
 
         def send(k, inner):
             back_copy(k).start()
@@ -236,44 +266,62 @@
         return carry
 
     lax.fori_loop(0, FF // FTILE, weights, 0)
-    pltpu.make_async_copy(return_buf, return_buf, back_recv_sem).wait()
+    upright[0] = tokens[...].T
+    upright[1] = upstream[...].T
+    router_flat[...] = router_rel[...].T
+    for i in range(2):
+        image = pl.ds(M * i, M)
+        flipped[0, :, image] = dispatch[image, :].T
+        flipped[1, :, image] = combine[image, :].T
     for g in range(GROUPS):
-        chunk = return_buf[GROUP * g : GROUP * (g + 1)].reshape(CHUNK, WIDTH)
-        split = dot(interleave[...], chunk, 0, 0).astype(BF16)
+        group = pl.ds(GROUP * g, GROUP)
+        pltpu.make_async_copy(
+            return_buf.at[group], return_buf.at[group], back_recv_sem.at[g]
+        ).wait()
+        split = dot(separate[...], return_buf[group].reshape(CHUNK, WIDTH)).astype(BF16)
         parts[:, 2 * GROUP * g : 2 * GROUP * (g + 1), :] = split.reshape(4, 2 * GROUP, WIDTH)
+        if g % 2 == 1:
+            slots = pl.ds(2 * GROUP * (g - 1), 4 * GROUP)
+            for i in range(2):
+                image = pl.ds(M * i, M)
+                grads[0, slots, image] = dot(parts[i, slots, :], upright[1, :, image])
+                grads[1, slots, image] = dot(parts[2 + i, slots, :], upright[0, :, image])
     lows = []
     for i in range(2):
         image = pl.ds(M * i, M)
-        disp = dispatch[image, :]
-        comb = combine[image, :]
-        combine_grad = dot(upstream[image, :], parts[i], 1, 1)
-        dispatch_grad = dot(tokens[image, :], parts[2 + i], 1, 1)
-        logit_grad = disp * (dispatch_grad - jnp.sum(disp * dispatch_grad, axis=0, keepdims=True))
+        disp = flipped[0, :, image]
+        comb = flipped[1, :, image]
+        combine_grad = grads[0, :, image]
+        dispatch_grad = grads[1, :, image]
+        logit_grad = disp * (dispatch_grad - jnp.sum(disp * dispatch_grad, axis=1, keepdims=True))
         logit_grad = logit_grad + comb * (
-            combine_grad - jnp.sum(comb * combine_grad, axis=1, keepdims=True)
+            combine_grad - jnp.sum(comb * combine_grad, axis=0, keepdims=True)
         )
         low = logit_grad.astype(BF16)
         lows.append(low)
-        logit_abs[image, :] = dot(low, turn[...], 1, 1).astype(BF16)
-    total = dot(tokens[...], logit_abs[...], 0, 0).astype(BF16)
-    terms[0] = total[:, :128]
-    terms[1] = total[:, 128:]
+        logit_abs[:, image] = dot(turn[...], low).astype(BF16)
 
     core = me % 2
     partner = device(me + 1 - 2 * core)
 
     pair = pltpu.make_async_remote_copy(
-        src_ref=terms.at[1 - core],
+        src_ref=terms,
         dst_ref=pair_in,
         send_sem=pair_sem.at[0],
         recv_sem=pair_sem.at[1],
         device_id=partner,
         device_id_type=MESH,
     )
+
+    def half(which):
+        return logit_abs[pl.ds(pl.multiple_of(which * 128, 128), 128), :]
+
+    terms[...] = dot(upright[0], half(1 - core), 1, 1).astype(BF16)
     pair.start()
+    own_terms = dot(upright[0], half(core), 1, 1)
     pair.wait_recv()
     chip_sum[...] = (
-        (terms[core].astype(F32) + pair_in[...].astype(F32)).astype(BF16).reshape(CHIPS, 16, 128)
+        (own_terms + pair_in[...].astype(F32)).astype(BF16).reshape(CHIPS, 16, 128)
     )
     pltpu.make_async_copy(chip_sum.at[me // 2], terms_in.at[0], term_sem.at[1]).start()
 
@@ -293,7 +341,7 @@
     for i in range(2):
         image = pl.ds(M * i, M)
         token_grad[image, :] = (
-            dot(dispatch[image, :].astype(BF16), parts[2 + i]) + dot(lows[i], router_rel[...], 1, 1)
+            dot(dispatch[image, :].astype(BF16), parts[2 + i]) + dot(lows[i], router_flat[...], 0, 0)
         ).astype(BF16)
 
     pltpu.make_async_copy(terms_in, terms_in, term_sem.at[1]).wait()
@@ -368,6 +416,7 @@
             vmem((WIDTH, SLOTS), BF16),
             vmem((SLOTS, SLOTS), BF16),
             vmem((CHUNK, CHUNK), BF16),
+            vmem((CHUNK, CHUNK), BF16),
             vmem((2 * M, SLOTS), F32),
             vmem((2 * M, SLOTS), F32),
             vmem((4, SLOTS, WIDTH), BF16),
@@ -381,8 +430,12 @@
             vmem((HALF, WIDTH), F32),
             vmem((N, ROWS, WIDTH), BF16),
             vmem((N, ROWS, WIDTH), BF16),
-            vmem((2 * M, SLOTS), BF16),
-            vmem((2, WIDTH, 128), BF16),
+            vmem((2, WIDTH, 2 * M), BF16),
+            vmem((SLOTS, WIDTH), BF16),
+            vmem((2, SLOTS, 2 * M), F32),
+            vmem((2, SLOTS, 2 * M), F32),
+            vmem((SLOTS, 2 * M), BF16),
+            vmem((WIDTH, 128), BF16),
             vmem((WIDTH, 128), BF16),
             vmem((CHIPS, 16, 128), BF16),
             vmem((CHIPS, 16, 128), BF16),
@@ -392,7 +445,7 @@
             dma,
             dma((GROUPS,)),
             dma,
-            dma,
+            dma((GROUPS,)),
             dma((2,)),
             dma((2,)),
             dma((2,)),

time: 86.6 us -> 86.4 us (level)
  no operation moved by 1% of the time
where the time goes in v4:
time: 86.4 us; the launch traced here: 86.2 us
  Pallas kernels  85.6 us (99%)
    pallas_call x1, Pallas kernels, local(): pl.pallas_call(kernel, out_shape=tuple((vmem(*shape) for shape in shapes)...  81.5 us
    pallas_call x1, Pallas kernels, local(): pl.pallas_call(store_kernel, out_shape=tuple((jax.ShapeDtypeStruct(*shape...  4.12 us

profile of v4, /device:TPU:1, one launch (start us, length us, event | category | flops | bytes accessed | tf_op | source)
XLA Modules:
  0.0 86.2 jit_solution(7343380066563253179)
XLA Ops:
  0.6 81.5 %shard_map.84 = (bf16[512,1024]{1,0:T(8,128)(2,1)S(1)}, f32[1024,256]{1,0:T(8,128)S(1)}, bf16[1,1024,2048]{2,1,0:T(8,128)(2,1)S(1)}, bf16[1,2048,1024]{2,1,0:T(8,128)(2,1)S(1)}) custom-call(bf16[512,1024]{1,0:T(8,128)(2,1)} %tokens_hbm.1, bf16[1024,256]{1,0:T(8,128)(2,1)} %router_hbm.1, bf16[1,1024,2048]{2,1,0:T(8,128)(2,1)} %first_hbm.1, ...), custom_call_target="tpu_custom_call" | custom-call | flops 16000000000 | bytes 12000000 | tf_op jit(solution)/shard_map/pallas_call | solution.py:405
  82.1 4.1 %shard_map.85 = (bf16[512,1024]{1,0:T(8,128)(2,1)}, f32[1024,256]{1,0:T(8,128)}, bf16[1,1024,2048]{2,1,0:T(8,128)(2,1)}, bf16[1,2048,1024]{2,1,0:T(8,128)(2,1)}) custom-call(bf16[512,1024]{1,0:T(8,128)(2,1)S(1)} %get-tuple-element.8.refs_0_, f32[1024,256]{1,0:T(8,128)S(1)} %get-tuple-element.9.refs_1_, bf16[1,1024,2048]{2,1,0:T(8,128)(2,1)S(1)} %get-tuple-element.10.refs_2_, ...), custom_call_target="tpu_custom_call" | custom-call | bytes 10000000 | tf_op jit(solution)/shard_map/pallas_call | solution.py:462

commit v5 on v4

--- a/solution.py
+++ b/solution.py
@@ -24,7 +24,7 @@
 CHUNK = GROUP * ROWS
 HALF = CHUNK // 2
 FTILE = 512
-STRIDE = 37
+STRIDE = 5
 
 root_two_pi = math.sqrt(2.0 / math.pi)
 cubic_coef = 0.044715

time: 86.4 us -> 85.5 us (0.990)
  no operation moved by 1% of the time
where the time goes in v5:
time: 85.5 us; the launch traced here: 85.4 us
  Pallas kernels  84.8 us (99%)
    pallas_call x1, Pallas kernels, local(): pl.pallas_call(kernel, out_shape=tuple((vmem(*shape) for shape in shapes)...  80.6 us
    pallas_call x1, Pallas kernels, local(): pl.pallas_call(store_kernel, out_shape=tuple((jax.ShapeDtypeStruct(*shape...  4.12 us

profile of v5, /device:TPU:1, one launch (start us, length us, event | category | flops | bytes accessed | tf_op | source)
XLA Modules:
  0.0 85.4 jit_solution(15198198615771905611)
XLA Ops:
  0.6 80.6 %shard_map.84 = (bf16[512,1024]{1,0:T(8,128)(2,1)S(1)}, f32[1024,256]{1,0:T(8,128)S(1)}, bf16[1,1024,2048]{2,1,0:T(8,128)(2,1)S(1)}, bf16[1,2048,1024]{2,1,0:T(8,128)(2,1)S(1)}) custom-call(bf16[512,1024]{1,0:T(8,128)(2,1)} %tokens_hbm.1, bf16[1024,256]{1,0:T(8,128)(2,1)} %router_hbm.1, bf16[1,1024,2048]{2,1,0:T(8,128)(2,1)} %first_hbm.1, ...), custom_call_target="tpu_custom_call" | custom-call | flops 16000000000 | bytes 12000000 | tf_op jit(solution)/shard_map/pallas_call | solution.py:405
  81.3 4.1 %shard_map.85 = (bf16[512,1024]{1,0:T(8,128)(2,1)}, f32[1024,256]{1,0:T(8,128)}, bf16[1,1024,2048]{2,1,0:T(8,128)(2,1)}, bf16[1,2048,1024]{2,1,0:T(8,128)(2,1)}) custom-call(bf16[512,1024]{1,0:T(8,128)(2,1)S(1)} %get-tuple-element.8.refs_0_, f32[1024,256]{1,0:T(8,128)S(1)} %get-tuple-element.9.refs_1_, bf16[1,1024,2048]{2,1,0:T(8,128)(2,1)S(1)} %get-tuple-element.10.refs_2_, ...), custom_call_target="tpu_custom_call" | custom-call | bytes 10000000 | tf_op jit(solution)/shard_map/pallas_call | solution.py:462
